TPU v7x, 32 devices: a whole 2x2x4 slice. The times are simulated.
32 devices in a mesh: facet: 8 (over y, x, core), bl: 4 (over z).
Axes of the slice: x: 2, y: 2, z: 4, core: 2. Of those that a mesh axis runs over, the one named last changes fastest.
Arguments:
- facet_model: bfloat16 [8, 1024, 1024], P('facet', 'bl'), may hold values from -0.005859375 to 0.005859375
- screens: bfloat16 [8, 256, 64, 128], P('facet', 'bl'), may hold values from 0.099609375 to 1.8984375
- observed: float32 [48, 64, 128], P('bl'), may hold values from -24 to 24
- offsets: int32 [48, 2], P('bl'), may hold values from 0 to 4032
- stations: int32 [48, 2], P('bl'), may hold values from 0 to 255
- counts: int32 [4], P('bl'), may hold values from 1 to 12, as said below
Outputs:
- residual_vis: float32 [48, 64, 128], P('bl')
- residual_image: float32 [8, 1024, 1024], P('facet', 'bl')
Inputs may be any that keep to these rules, and one draw needn't show every extreme that they name: `counts`: some baseline block has all 12 slots live.
All inputs are finite; a program needn't handle non-finite values.
Results may differ from a plain program's by a relative error of at most 0.0061.
Values may be sent and summed in bfloat16 or wider, within the bound.
A program may use at most 64 MiB of HBM per device.

v0:
```python
import math

import jax
import jax.numpy as jnp
from jax import lax
from jax.sharding import PartitionSpec as P

FGRID = 4


def tables(offset_u, offset_v, facet_id, tile_width, facet_cells):
    grid_cells = FGRID * facet_cells
    corner_x = facet_id // FGRID * facet_cells
    corner_y = facet_id % FGRID * facet_cells
    pixel_index = jnp.arange(facet_cells, dtype=jnp.int32)
    cell_index = jnp.arange(tile_width, dtype=jnp.int32)
    phase_u = jnp.mod(
        (offset_u + cell_index)[:, None] * (corner_x + pixel_index)[None, :], grid_cells
    )
    phase_v = jnp.mod(
        (offset_v + cell_index)[:, None] * (corner_y + pixel_index)[None, :], grid_cells
    )
    angle_u = phase_u.astype(jnp.float32) * (2.0 * math.pi / grid_cells)
    angle_v = phase_v.astype(jnp.float32) * (2.0 * math.pi / grid_cells)
    tab_u = jnp.concatenate([jnp.cos(angle_u), -jnp.sin(angle_u)], axis=0).astype(jnp.bfloat16)
    table_vertical = jnp.concatenate([jnp.cos(angle_v), jnp.sin(angle_v)], axis=0).astype(
        jnp.bfloat16
    )
    return (tab_u, table_vertical)


def half_splits(value):
    half_width = value.shape[-1] // 2
    return (value[..., :half_width], value[..., half_width:])


def complex_times(left_re, left_im, right_re, right_im):
    return (left_re * right_re - left_im * right_im, left_re * right_im + left_im * right_re)


def times_conj(left_re, left_im, right_re, right_im):
    return (left_re * right_re + left_im * right_im, left_im * right_re - left_re * right_im)


def per_device(facet_model, screens, observed, offsets, stations, counts):
    tile_count = observed.shape[0]
    tile_width = observed.shape[1]
    facet_cells = facet_model.shape[2]
    bl_devices = lax.axis_size("bl")
    facet_id = lax.axis_index("facet")
    make_tables = jax.vmap(tables, in_axes=(0, 0, None, None, None))
    tab_u, table_vertical = make_tables(
        offsets[:, 0], offsets[:, 1], facet_id, tile_width, facet_cells
    )
    upper_portion = jnp.einsum(
        "tkn,np->tkp",
        tab_u,
        lax.all_gather(facet_model[0], "bl", axis=0, tiled=True),
        preferred_element_type=jnp.float32,
    ).astype(jnp.bfloat16)
    block_groups = jnp.einsum(
        "gsf,gmf->gsm", upper_portion, table_vertical, preferred_element_type=jnp.float32
    )
    real_part = (
        block_groups[:, :tile_width, :tile_width] + block_groups[:, tile_width:, tile_width:]
    )
    imag_part = (
        block_groups[:, tile_width:, :tile_width] - block_groups[:, :tile_width, tile_width:]
    )
    all_screens = lax.all_gather(screens[0], "bl", axis=0, tiled=True)
    first_station_gain = jnp.take(all_screens, stations[:, 0], axis=0).astype(jnp.float32)
    gain_q = jnp.take(all_screens, stations[:, 1], axis=0).astype(jnp.float32)
    p_re, p_im = half_splits(first_station_gain)
    q_re, q_im = half_splits(gain_q)
    y_re, y_im = complex_times(p_re, p_im, real_part, imag_part)
    x_re, x_im = times_conj(y_re, y_im, q_re, q_im)
    contribution = jnp.concatenate([x_re, x_im], axis=2)
    live_mask = (jnp.arange(tile_count, dtype=jnp.int32) < counts[0])[:, None, None]
    predicted = lax.psum(contribution, "facet")
    residual = jnp.where(live_mask, observed - predicted, jnp.zeros_like(observed))
    r_re, r_im = half_splits(residual)
    z_re, z_im = times_conj(r_re, r_im, p_re, p_im)
    w_re, w_im = complex_times(z_re, z_im, q_re, q_im)
    w_re = w_re.astype(jnp.bfloat16)
    w_im = w_im.astype(jnp.bfloat16)
    stacked = jnp.concatenate(
        [jnp.concatenate([w_re, -w_im], axis=2), jnp.concatenate([w_im, w_re], axis=2)], axis=1
    )
    q_two = jnp.einsum(
        "tuk,tky->tuy", stacked, table_vertical, preferred_element_type=jnp.float32
    ).astype(jnp.bfloat16)
    image_scale = 1.0 / (32.0 * tile_width * math.sqrt(tile_count * bl_devices))
    row_count = facet_cells // bl_devices
    whole_image = jnp.einsum("tkx,tky->xy", tab_u, q_two, preferred_element_type=jnp.float32)
    summed = lax.psum(whole_image, "bl")
    own_rows = lax.dynamic_slice_in_dim(summed, lax.axis_index("bl") * row_count, row_count, 0)
    residual_image = (own_rows * image_scale)[None]
    return (residual, residual_image)


def solution(mesh):
    in_specs = (
        P("facet", "bl", None),
        P("facet", "bl", None, None),
        P("bl", None, None),
        P("bl", None),
        P("bl", None),
        P("bl"),
    )
    out_specs = (P("bl", None, None), P("facet", "bl", None))
    return jax.shard_map(
        per_device, mesh=mesh, in_specs=in_specs, out_specs=out_specs, check_vma=False
    )
```

profile of v0, /device:TPU:0, one launch (start us, length us, event | category | flops | bytes accessed | tf_op | source)
XLA Modules:
  0.0 373.6 jit_solution(2126183695265886717)
XLA Ops:
  7.2 0.0 all-gather.7.cloned.1.call-start
  7.2 0.7 all-gather.7.cloned.1.call-update
  7.9 0.0 all-gather.5.cloned.1.call-start
  7.9 0.7 all-gather.5.cloned.1.call-update
  8.6 0.0 all-reduce.3.cloned.1.call-start
  8.7 0.8 compare_and_fusion.1
  9.5 0.8 slice_bitcast_fusion.1
  10.3 0.1 iota_add_fusion
  10.4 14.1 %cosine_convert_fusion = (bf16[12,64,1024]{2,1,0:T(8,128)(2,1)S(1)}, bf16[12,64,1024]{2,1,0:T(8,128)(2,1)}) fusion(s32[1024]{0:T(1024)S(1)} %iota_add_fusion.2, s32[12,64]{1,0:T(8,128)S(1)} %get-tuple-element.24), kind=kLoop, calls=%fused_computation.23 | loop fusion | flops 12582912 | bytes 3152896 | tf_op jit(solution)/shard_map/convert
  24.4 14.2 %cosine_convert_fusion.1 = (bf16[12,64,1024]{2,1,0:T(8,128)(2,1)}, bf16[12,64,1024]{2,1,0:T(8,128)(2,1)}) fusion(s32[1024]{0:T(1024)S(1)} %iota_add_fusion.3, s32[12,64]{1,0:T(8,128)S(1)} %get-tuple-element.25), kind=kLoop, calls=%fused_computation.27 | loop fusion | flops 13369344 | bytes 3152896 | tf_op jit(solution)/shard_map/convert.2
  38.6 19.7 %all-gather.7.cloned.1.call-done = bf16[1,1024,1024]{2,1,0:T(8,128)(2,1)} async-done(((bf16[1,256,1024]{2,1,0:T(8,128)(2,1)}), bf16[1,1024,1024]{2,1,0:T(8,128)(2,1)}) %all-gather.7.cloned.1.call-update) | async-done | bytes 2097168 | tf_op jit(solution)/shard_map/all_gather | solution.py:58
  58.4 7.2 %fusion.8 = f32[12,128,128]{2,1,0:T(8,128)S(1)} fusion(bf16[12,64,1024]{2,1,0:T(8,128)(2,1)} %get-tuple-element.17, bf16[12,64,1024]{2,1,0:T(8,128)(2,1)S(1)} %get-tuple-element.16, bf16[1,1024,1024]{2,1,0:T(8,128)(2,1)} %all-gather.7.cloned.1.call-done, bf16[12,64,1024]{2,1,0:T(8,128)(2,1)} %get-tuple-element.15, bf16[12,64,1024]{2,1,0:T(8,128)(2,1)} %get-tuple-element.14), kind=kOutput, calls=%fused_computation.24 | convolution fusion | flops 3638034432 | bytes 9175040 | tf_op jit(solution)/shard_map/gsf,gmf->gsm/dot_general | solution.py:61
  65.6 74.1 %all-gather.5.cloned.1.call-done = bf16[1,256,64,128]{3,2,0,1:T(8,128)(2,1)} async-done(((bf16[1,64,64,128]{3,2,0,1:T(8,128)(2,1)}), bf16[1,256,64,128]{3,2,0,1:T(8,128)(2,1)}) %all-gather.5.cloned.1.call-update) | async-done | bytes 4194320 | tf_op jit(solution)/shard_map/all_gather | solution.py:70
  139.7 2.8 gather_fusion.1
  142.5 2.8 gather_fusion
  145.3 0.1 select_convert_fusion
  145.4 0.0 copy-start.1
  145.4 0.5 multiply_add_fusion.1
  145.9 0.2 multiply_subtract_fusion.1
  146.1 0.9 pad_maximum_fusion.11
  147.0 0.0 all-reduce.3.cloned.1.call-update
  147.0 0.2 all-reduce.5.cloned.1.call-start
  147.9 51.9 %all-reduce.3.cloned.1.call-done = f32[12,64,128]{2,1,0:T(8,128)} async-done(((f32[12,64,128]{2,1,0:T(8,128)}), f32[12,64,128]{2,1,0:T(8,128)}) %all-reduce.3.cloned.1.call-update) | async-done | bytes 393232 | tf_op jit(solution)/shard_map/psum | solution.py:79
  199.9 0.0 copy-done.1
  199.9 1.1 subtract_select_fusion
  201.0 0.0 copy-start
  201.0 0.4 fusion.39
  201.4 0.2 subtract_convert_fusion
  201.6 8.6 %fusion.12 = f32[1024,1024]{1,0:T(8,128)} fusion(bf16[12,64,1024]{2,1,0:T(8,128)(2,1)} %get-tuple-element.17, bf16[12,64,1024]{2,1,0:T(8,128)(2,1)S(1)} %get-tuple-element.16, bf16[12,64,1024]{2,1,0:T(8,128)(2,1)} %get-tuple-element.15, bf16[12,64,1024]{2,1,0:T(8,128)(2,1)} %get-tuple-element.14, bf16[12,64,64]{2,1,0:T(8,128)(2,1)S(1)} %subtract_convert_fusion, ...), kind=kOutput, calls=%fused_computation.29 | convolution fusion | flops 3639607296 | bytes 10780672 | tf_op jit(solution)/shard_map/tkx,tky->xy/dot_general | solution.py:94
  210.2 0.0 copy-done
  210.2 0.0 all-reduce.5.cloned.1.call-update
  210.2 154.4 %all-reduce.5.cloned.1.call-done = f32[1024,1024]{1,0:T(8,128)} async-done(((f32[1024,1024]{1,0:T(8,128)}), f32[1024,1024]{1,0:T(8,128)}) %all-reduce.5.cloned.1.call-update) | async-done | bytes 4194320 | tf_op jit(solution)/shard_map/psum | solution.py:95
  364.7 2.3 multiply_bitcast_fusion
  (5 shorter events, 0.0 us)
Async XLA Ops:
  7.2 51.2 %all-gather.7.cloned.1.call-start = ((), (), s32[]{:S(2)}) async-start(), calls=%async_computation.3 | async-start | bytes 2621440 | tf_op jit(solution)/shard_map/all_gather | solution.py:58
  7.9 131.8 %all-gather.5.cloned.1.call-start = ((), (), s32[]{:S(2)}) async-start(), calls=%async_computation.2 | async-start | bytes 5242880 | tf_op jit(solution)/shard_map/all_gather | solution.py:70
  8.6 191.2 %all-reduce.3.cloned.1.call-start = ((), (), s32[]{:S(2)}) async-start(), calls=%async_computation | async-start | bytes 786432 | tf_op jit(solution)/shard_map/psum | solution.py:79
  145.4 54.5 %copy-start.1 = (f32[12,64,128]{2,1,0:T(8,128)S(1)}, f32[12,64,128]{2,1,0:T(8,128)}, u32[]{:S(2)}) copy-start(f32[12,64,128]{2,1,0:T(8,128)} %param.10) | copy-start | bytes 1179652
  147.0 217.7 %all-reduce.5.cloned.1.call-start = ((), (), s32[]{:S(2)}) async-start(), calls=%async_computation.1 | async-start | bytes 8388608 | tf_op jit(solution)/shard_map/psum | solution.py:95
  201.0 9.2 %copy-start = (f32[12,64,128]{2,1,0:T(8,128)}, f32[12,64,128]{2,1,0:T(8,128)S(1)}, u32[]{:S(2)}) copy-start(f32[12,64,128]{2,1,0:T(8,128)S(1)} %subtract_select_fusion) | copy-start | bytes 1179652
Sparse Core Ops, SparseCore 0:
  9.6 48.7 all-gather.6
  59.9 79.7 all-gather.4
  147.1 52.6 all-reduce.2
  210.4 154.2 all-reduce.4
where the time goes:
time: 374 us
  waiting for transfers between devices  302 us (81%)
  other arithmetic  34.9 us (9%)
  matrix products  15.9 us (4%)
  between operations  14.5 us (4%)
  local copies, waits for them, and re-layouts  6.31 us (2%)
    psum x1, waiting for transfers between devices, per_device(): summed = lax.psum(whole_image, 'bl')  154 us
    all_gather x1, waiting for transfers between devices, per_device(): all_screens = lax.all_gather(screens[0], 'bl', axis=0, tiled=True)  74.1 us
    psum x1, waiting for transfers between devices, per_device(): predicted = lax.psum(contribution, 'facet')  51.9 us
    another operation x2, other arithmetic  28.3 us
    all_gather x1, waiting for transfers between devices, per_device(): lax.all_gather(facet_model[0], 'bl', axis=0, tiled=True)  19.7 us
    dot_general x1, matrix products, per_device(): jnp.einsum('tkx,tky->xy', tab_u, q_two, preferred_element_type=jnp.float32)  8.64 us
  transfers between devices with their start and end apart: 4, of which 4 were waited for; matrix products, arithmetic and copies ran while one was open for 10% of the time, Pallas kernels for 0%

commit v1 on v0

v1 whole, which is shorter than its diff:
```python
import functools
import math

import jax
import jax.numpy as jnp
from jax import lax
from jax.experimental import pallas as pl
from jax.experimental.pallas import tpu as pltpu
from jax.sharding import PartitionSpec as P

FGRID = 4
F32 = jnp.float32
BF16 = jnp.bfloat16


def cis(k, cells):
    shift = (cells // 4).bit_length() - 1
    turn = (k + cells // 8) >> shift
    x = (k - (turn << shift)).astype(F32) * (2.0 * math.pi / cells)
    y = x * x
    s = x * (1.0 + y * (-1.0 / 6 + y * (1.0 / 120 + y * (-1.0 / 5040 + y * (1.0 / 362880)))))
    c = 1.0 + y * (-0.5 + y * (1.0 / 24 + y * (-1.0 / 720 + y * (1.0 / 40320))))
    odd = (turn & 1) == 1
    cos = jnp.where(odd, s, c)
    sin = jnp.where(odd, c, s)
    cos = jnp.where(((turn + 1) & 2) == 2, -cos, cos)
    sin = jnp.where((turn & 2) == 2, -sin, sin)
    return cos, sin


def kernel(
    dims,
    meta_ref,
    model_ref,
    screens_ref,
    obs_ref,
    image_ref,
    resout_ref,
    meta_land,
    meta_all,
    e2u,
    e1u,
    e1v,
    wv,
    tabu,
    scr_land,
    sbuf,
    s_land,
    sown,
    gbuf,
    cbuf,
    c_land,
    obs_land,
    obsfull,
    livefull,
    res16,
    r_land,
    rall,
    zsend,
    reso,
    z_send,
    z_recv,
    p_send,
    p_recv,
    own_sem,
):
    F, B, T, TD, G, PX, rows, Uc, UB, RPF, nu, per = dims
    N = FGRID * PX
    f = lax.axis_index("facet")
    me = lax.axis_index("bl")
    spd = screens_ref.shape[1]
    UBT = UB * T
    H = G

    barrier = pltpu.get_barrier_semaphore()
    for k in range(1, B):
        pl.semaphore_signal(
            barrier, inc=1, device_id={"bl": lax.rem(me + k, B)},
            device_id_type=pl.DeviceIdType.MESH,
        )
    for k in range(1, F):
        pl.semaphore_signal(
            barrier, inc=1, device_id={"facet": lax.rem(f + k, F)},
            device_id_type=pl.DeviceIdType.MESH,
        )

    def zcopy(stage, k, src, dst):
        return pltpu.make_async_remote_copy(
            src_ref=src, dst_ref=dst, send_sem=z_send.at[stage, k], recv_sem=z_recv.at[stage, k],
            device_id={"bl": lax.rem(me + k, B)}, device_id_type=pl.DeviceIdType.MESH,
        )

    def pcopy(stage, k, src, dst):
        return pltpu.make_async_remote_copy(
            src_ref=src, dst_ref=dst, send_sem=p_send.at[stage, k], recv_sem=p_recv.at[stage, k],
            device_id={"facet": lax.rem(f + k, F)}, device_id_type=pl.DeviceIdType.MESH,
        )

    def scr_rows(s):
        return pl.ds(pl.multiple_of(s * spd, spd), spd)

    corner_x = (f // FGRID) * PX
    corner_y = (f % FGRID) * PX
    pix_u = lax.broadcasted_iota(jnp.int32, (1, rows), 1) + (corner_x + me * rows)
    pix_v = lax.broadcasted_iota(jnp.int32, (1, PX), 1) + corner_y

    pl.semaphore_wait(barrier, B + F - 2)

    meta_copies = [zcopy(0, k, meta_ref, meta_land.at[me]) for k in range(1, B)]
    obs_copies = []
    scr_copies = []
    for k in range(1, B):
        c = lax.rem(me + k, B)
        u0 = c * Uc + (f // per) * nu
        obs_copies.append(zcopy(1, k, obs_ref.at[pl.ds(u0, nu)], obs_land.at[me]))
        scr_copies.append(
            zcopy(2, k, screens_ref.at[pl.ds(c * Uc, Uc)], scr_land.at[:, scr_rows(me)])
        )
    for group in (meta_copies, obs_copies, scr_copies):
        for copy in group:
            copy.start()
    own_copy = pltpu.make_async_copy(
        screens_ref.at[pl.ds(me * Uc, Uc)], scr_land.at[:, scr_rows(me)], own_sem
    )
    own_copy.start()
    meta_land[me] = meta_ref[...]
    obs_land[me] = obs_ref[pl.ds(me * Uc + (f // per) * nu, nu)]

    cells = lax.broadcasted_iota(jnp.int32, (G, 1), 0)
    cu, su = cis(cells * pix_u, N)
    e2u[0] = cu
    e2u[1] = su
    for j in range(0, PX, 256):
        cv, sv = cis(cells * pix_v[:, j : j + 256], N)
        wv[:H, j : j + 256] = cv.astype(BF16)
        wv[H:, j : j + 256] = sv.astype(BF16)

    for copy in meta_copies:
        copy.wait()
    for b in range(B):
        meta_all[b * TD : (b + 1) * TD, :] = meta_land[b, :TD, :]
    ou = meta_all[:, 0:1]
    ov = meta_all[:, 1:2]
    c1, s1 = cis(ou * pix_u, N)
    e1u[0] = c1
    e1u[1] = s1
    for j in range(0, PX, 256):
        c1, s1 = cis(ov * pix_v[:, j : j + 256], N)
        e1v[0, :, j : j + 256] = c1
        e1v[1, :, j : j + 256] = s1

    lane = lax.broadcasted_iota(jnp.int32, (1, 2 * G), 1)
    left = lane < G
    sgn = jnp.where(left, 1.0, -1.0).astype(F32)

    def swap(x):
        return pltpu.roll(x, G, 1)

    nchunk = Uc // UB

    def predict(c, i):
        ci = c * nchunk + i
        for j in range(UB):
            u = c * Uc + i * UB + j
            e2c = e2u[0, pl.ds(u, 1), :]
            e2s = e2u[1, pl.ds(u, 1), :]
            a_c = e1u[0]
            a_s = e1u[1]
            tabu[ci, j * T : (j + 1) * T, :] = (a_c * e2c - a_s * e2s).astype(BF16)
            tabu[ci, UBT + j * T : UBT + (j + 1) * T, :] = (-(a_s * e2c + a_c * e2s)).astype(BF16)
        up = jnp.dot(tabu[ci], model_ref[...], preferred_element_type=F32)
        tops, bots = [], []
        for j in range(UB):
            uc = up[j * T : (j + 1) * T]
            us = up[UBT + j * T : UBT + (j + 1) * T]
            tops.append((uc * e1v[0] + us * e1v[1]).astype(BF16))
            bots.append((us * e1v[0] - uc * e1v[1]).astype(BF16))
        both = jnp.concatenate(tops + bots, axis=0)
        b = lax.dot_general(
            both, wv[...], (((1,), (1,)), ((), ())), preferred_element_type=F32
        )
        return b[:UBT] * sgn + swap(b[UBT:])

    s_copies = []
    for k in range(1, B):
        c = lax.rem(me + k, B)

        def body(i, carry, c=c):
            rows_i = pl.ds(pl.multiple_of(i * UBT, UBT), UBT)
            sbuf[c, rows_i, :] = predict(c, i).astype(BF16)
            return carry

        lax.fori_loop(0, nchunk, body, 0)
        copy = zcopy(3, k, sbuf.at[c], s_land.at[me])
        copy.start()
        s_copies.append(copy)

    def body_own(i, carry):
        rows_i = pl.ds(pl.multiple_of(i * UBT, UBT), UBT)
        sown[rows_i, :] = predict(me, i)
        return carry

    lax.fori_loop(0, nchunk, body_own, 0)

    for copy in obs_copies:
        copy.wait()
    for j in range(nu):
        for b in range(B):
            obsfull[j * T + b * TD : j * T + (b + 1) * TD, :] = obs_land[b, j]
        livefull[j * T : (j + 1) * T, :] = jnp.broadcast_to(
            meta_all[:, 4:5].astype(F32), (T, 2 * G)
        )

    own_copy.wait()
    for copy in scr_copies:
        copy.wait()
    stations = lax.broadcasted_iota(jnp.int32, (1, B * spd), 1)
    pick = jnp.concatenate([meta_all[:, 2:3], meta_all[:, 3:4]], axis=0) == stations
    pick = jnp.where(pick, 1.0, 0.0).astype(BF16)

    def gains(u, carry):
        both = jnp.dot(pick, scr_land[u], preferred_element_type=F32)
        p = both[:T]
        q = both[T:]
        qsw = swap(q)
        g = p * jnp.where(left, q, qsw) + swap(p) * jnp.where(left, qsw, -q)
        gbuf[pl.ds(pl.multiple_of(u * T, T), T), :] = g
        return carry

    lax.fori_loop(0, Uc, gains, 0)

    for copy in s_copies:
        copy.wait()

    def contribution(u, carry):
        r = pl.ds(pl.multiple_of(u * T, T), T)
        s = sown[r, :]
        for k in range(1, B):
            s = s + s_land[lax.rem(me + k, B), r, :].astype(F32)
        g = gbuf[r, :]
        gsw = swap(g)
        out = s * jnp.where(left, g, gsw) + swap(s) * jnp.where(left, -gsw, g)
        cbuf[r, :] = out.astype(BF16)
        return carry

    lax.fori_loop(0, Uc, contribution, 0)

    def piece(i):
        return pl.ds(pl.multiple_of(i * RPF, RPF), RPF)

    c_copies = [
        pcopy(0, k, cbuf.at[piece(lax.rem(f + k, F))], c_land.at[f]) for k in range(1, F)
    ]
    for copy in c_copies:
        copy.start()
    total = cbuf[piece(f), :].astype(F32)
    for copy in c_copies:
        copy.wait()
    for k in range(1, F):
        total = total + c_land[lax.rem(f + k, F)].astype(F32)
    span = pl.ds(pl.multiple_of((f % per) * RPF, RPF), RPF)
    res = jnp.where(livefull[span, :] > 0.5, obsfull[span, :] - total, 0.0)
    r_land[piece(f), :] = res.astype(BF16)
    res16[...] = res.astype(BF16)
    r_copies = [pcopy(1, k, res16, r_land.at[piece(f)]) for k in range(1, F)]
    for copy in r_copies:
        copy.start()
    if per > 1:
        obsfull[...] = jnp.zeros_like(obsfull)
    obsfull[span, :] = res
    for j in range(nu):
        for b in range(B):
            zsend[b, j] = obsfull[j * T + b * TD : j * T + (b + 1) * TD, :]
    reso[f, me] = zsend[me]
    for copy in r_copies:
        copy.wait()

    def weigh(u, carry):
        r = pl.ds(pl.multiple_of(u * T, T), T)
        x = r_land[r, :].astype(F32)
        g = gbuf[r, :]
        gsw = swap(g)
        out = x * jnp.where(left, g, gsw) + swap(x) * jnp.where(left, gsw, -g)
        rall[me, r, :] = out.astype(BF16)
        return carry

    lax.fori_loop(0, Uc, weigh, 0)
    w_copies = [zcopy(4, k, rall.at[me], rall.at[me]) for k in range(1, B)]
    for copy in w_copies:
        copy.start()
    z_copies = [
        zcopy(5, k, zsend.at[lax.rem(me + k, B)], reso.at[f, me]) for k in range(1, B)
    ]
    for copy in z_copies:
        copy.start()

    image_ref[...] = jnp.zeros_like(image_ref)

    def image(src):
        def body(i, carry):
            ci = src * nchunk + i
            r = rall[src, pl.ds(pl.multiple_of(i * UBT, UBT), UBT), :].astype(F32)
            both = jnp.concatenate([(r * sgn).astype(BF16), swap(r).astype(BF16)], axis=0)
            prod = jnp.dot(both, wv[...], preferred_element_type=F32)
            tops, bots = [], []
            for j in range(UB):
                pc = prod[j * T : (j + 1) * T]
                ps = prod[UBT + j * T : UBT + (j + 1) * T]
                tops.append((pc * e1v[0] - ps * e1v[1]).astype(BF16))
                bots.append((ps * e1v[0] + pc * e1v[1]).astype(BF16))
            q2 = jnp.concatenate(tops + bots, axis=0)
            image_ref[...] += lax.dot_general(
                tabu[ci], q2, (((0,), (0,)), ((), ())), preferred_element_type=F32
            )
            return carry

        lax.fori_loop(0, nchunk, body, 0)

    image(me)
    for copy in z_copies:
        copy.wait()
    o_copies = [pcopy(2, k, reso.at[f], reso.at[f]) for k in range(1, F)]
    for copy in o_copies:
        copy.start()
    for k in range(1, B):
        w_copies[k - 1].wait()
        image(lax.rem(me + B - k, B))
    image_ref[...] = image_ref[...] * (1.0 / (32.0 * G * math.sqrt(T)))
    for copy in o_copies:
        copy.wait()
    resout_ref[...] = reso[...]


def per_device(F, B, facet_model, screens, observed, offsets, stations, counts):
    TD, G = observed.shape[0], observed.shape[1]
    PX = facet_model.shape[2]
    rows = facet_model.shape[1]
    spd = screens.shape[1]
    T = TD * B
    Uc = G // B
    UB = max(1, min(Uc, 192 // T))
    RPF = Uc * T // F
    nu = max(1, RPF // T)
    per = max(1, T // RPF)
    dims = (F, B, T, TD, G, PX, rows, Uc, UB, RPF, nu, per)
    tdp = -(-TD // 8) * 8
    live = (jnp.arange(TD, dtype=jnp.int32) < counts[0]).astype(jnp.int32)[:, None]
    meta = jnp.concatenate([offsets, stations, live], axis=1)
    meta = jnp.pad(meta, ((0, tdp - TD), (0, 128 - meta.shape[1])))
    screens_t = jnp.transpose(screens[0], (1, 0, 2))
    obs_t = jnp.transpose(observed, (1, 0, 2))
    W = 2 * G
    vmem = pl.BlockSpec(memory_space=pltpu.VMEM)
    image, res = pl.pallas_call(
        functools.partial(kernel, dims),
        out_shape=(
            jax.ShapeDtypeStruct((rows, PX), F32),
            jax.ShapeDtypeStruct((F, B, nu, TD, W), F32),
        ),
        in_specs=[vmem] * 4,
        out_specs=(vmem, vmem),
        scratch_shapes=[
            pltpu.VMEM((B, tdp, 128), jnp.int32),
            pltpu.VMEM((T, 128), jnp.int32),
            pltpu.VMEM((2, G, rows), F32),
            pltpu.VMEM((2, T, rows), F32),
            pltpu.VMEM((2, T, PX), F32),
            pltpu.VMEM((W, PX), BF16),
            pltpu.VMEM((G // UB, 2 * UB * T, rows), BF16),
            pltpu.VMEM((Uc, B * spd, W), BF16),
            pltpu.VMEM((B, Uc * T, W), BF16),
            pltpu.VMEM((B, Uc * T, W), BF16),
            pltpu.VMEM((Uc * T, W), F32),
            pltpu.VMEM((Uc * T, W), F32),
            pltpu.VMEM((Uc * T, W), BF16),
            pltpu.VMEM((F, RPF, W), BF16),
            pltpu.VMEM((B, nu, TD, W), F32),
            pltpu.VMEM((nu * T, W), F32),
            pltpu.VMEM((nu * T, W), F32),
            pltpu.VMEM((RPF, W), BF16),
            pltpu.VMEM((Uc * T, W), BF16),
            pltpu.VMEM((B, Uc * T, W), BF16),
            pltpu.VMEM((B, nu, TD, W), F32),
            pltpu.VMEM((F, B, nu, TD, W), F32),
            pltpu.SemaphoreType.DMA((6, B)),
            pltpu.SemaphoreType.DMA((6, B)),
            pltpu.SemaphoreType.DMA((3, F)),
            pltpu.SemaphoreType.DMA((3, F)),
            pltpu.SemaphoreType.DMA,
        ],
        compiler_params=pltpu.CompilerParams(
            collective_id=0, has_side_effects=True, vmem_limit_bytes=56 * 1024 * 1024
        ),
    )(meta, facet_model[0], screens_t, obs_t)
    group = lax.axis_index("bl") * TD // RPF if per > 1 else 0
    res = res.reshape(F // per, per, B, nu, TD, W)
    res = lax.dynamic_index_in_dim(res, group, axis=1, keepdims=False)
    res = jnp.transpose(res, (3, 1, 0, 2, 4)).reshape(TD, G, W)
    return (res, image[None])


def solution(mesh):
    in_specs = (
        P("facet", "bl", None),
        P("facet", "bl", None, None),
        P("bl", None, None),
        P("bl", None),
        P("bl", None),
        P("bl"),
    )
    out_specs = (P("bl", None, None), P("facet", "bl", None))
    return jax.shard_map(
        functools.partial(per_device, mesh.shape["facet"], mesh.shape["bl"]),
        mesh=mesh, in_specs=in_specs, out_specs=out_specs, check_vma=False,
    )
```

time: 374 us -> 103 us (0.28)
  waiting for transfers between devices: 302 us -> 0 us
  Pallas kernels: 0 us -> 90.3 us
  other arithmetic: 34.9 us -> 0.09 us
  matrix products: 15.9 us -> 0 us
  between operations: 14.5 us -> 1.3 us
  local copies, waits for them, and re-layouts: 6.31 us -> 11.2 us
    psum x2 -> x0, waiting for transfers between devices: 206 us -> none  [the longest x1 154 us: per_device(): summed = lax.psum(whole_image, 'bl')]
    all_gather x2 -> x0, waiting for transfers between devices: 93.8 us -> none  [the longest x1 74.1 us: per_device(): all_screens = lax.all_gather(screens[0], 'bl', axis=0, tiled=True)]
    pallas_call x0 -> x1, Pallas kernels: none -> 90.3 us  [per_device(): pl.pallas_call(functools.partial(kernel, dims), out_shape=(jax.ShapeDtype...]
    another operation x2 -> x0, other arithmetic: 28.3 us -> none
    dot_general x2 -> x0, matrix products: 15.9 us -> none  [the longest x1 8.64 us: per_device(): jnp.einsum('tkx,tky->xy', tab_u, q_two, preferred_element_type=jnp.float32)]
    unnamed x4 -> x9, local copies, waits for them, and re-layouts: 0.01 us -> 8.64 us
    gather x2 -> x0, local copies, waits for them, and re-layouts: 5.54 us -> none  [the longest x1 2.77 us: per_device(): jnp.take(all_screens, stations[:, 0], axis=0).astype(jnp.float32)]
  transfers between devices with their start and end apart: 4 -> 0, of which waited for: 4 -> 0; matrix products, arithmetic and copies ran while one was open for 10% -> 0% of each run, Pallas kernels for 0% -> 0%
where the time goes in v1:
time: 103 us
  Pallas kernels  90.3 us (88%)
  local copies, waits for them, and re-layouts  11.2 us (11%)
  between operations  1.3 us (1%)
    pallas_call x1, Pallas kernels, per_device(): pl.pallas_call(functools.partial(kernel, dims), out_shape=(jax.ShapeDtype...  90.3 us
    unnamed x9, local copies, waits for them, and re-layouts  8.64 us

profile of v1, /device:TPU:0, one launch (start us, length us, event | category | flops | bytes accessed | tf_op | source)
XLA Modules:
  0.0 102.9 jit_solution(13369470982497051126)
XLA Ops:
  1.3 0.0 copy-start
  1.3 0.7 copy-done
  2.0 0.0 copy-start.1
  2.0 0.1 copy.12
  2.1 0.6 copy-done.1
  2.6 0.1 copy.13
  2.7 0.1 pad_add_fusion
  2.8 0.6 pad.4.meta_ref
  3.4 2.0 %copy.20 = f32[12,64,128]{2,0,1:T(8,128)} copy(f32[12,64,128]{2,1,0:T(8,128)} %param.8) | data formatting | bytes 786432 | tf_op args[2]
  5.4 2.9 %copy.19 = bf16[1,64,64,128]{3,1,2,0:T(8,128)(2,1)} copy(bf16[1,64,64,128]{3,2,1,0:T(8,128)(2,1)} %param.7) | data formatting | bytes 2097152 | tf_op args[1]
  8.3 90.3 %shard_map.77 = (f32[256,1024]{1,0:T(8,128)}, f32[8,4,2,12,128]{4,3,2,1,0:T(8,128)}) custom-call(s32[16,128]{1,0:T(8,128)} %pad.4.meta_ref, bf16[256,1024]{1,0:T(8,128)(2,1)} %bitcast.18, bf16[64,64,128]{2,1,0:T(8,128)(2,1)} %bitcast.14, f32[64,12,128]{2,1,0:T(8,128)} %bitcast.15), custom_call_target="tpu_custom_call" | custom-call | tf_op jit(solution)/shard_map/pallas_call | solution.py:354
  98.6 2.0 %copy.16 = f32[12,4,8,2,128]{4,3,2,1,0:T(2,128)} copy(f32[12,4,8,2,128]{4,0,3,1,2:T(8,128)} %bitcast.17) | data formatting | bytes 786432 | tf_op jit(solution)/shard_map/transpose | solution.py:398
  100.6 2.3 %copy.23 = f32[1,256,1024]{2,1,0:T(8,128)} copy(f32[1,256,1024]{2,1,0:T(8,128)} %bitcast.16) | data formatting | bytes 2097152
  (1 shorter events, 0.0 us)
Async XLA Ops:
  1.3 0.7 copy-start
  2.0 0.7 copy-start.1

commit v2 on v1

--- a/solution.py
+++ b/solution.py
@@ -30,13 +30,17 @@
 
 def kernel(
     dims,
-    meta_ref,
+    offsets_ref,
+    stations_ref,
+    counts_ref,
     model_ref,
     screens_ref,
     obs_ref,
     image_ref,
-    resout_ref,
+    pred_ref,
+    meta_ref,
     meta_land,
+    osend,
     meta_all,
     e2u,
     e1u,
@@ -62,6 +66,8 @@
     z_recv,
     p_send,
     p_recv,
+    w_send,
+    w_recv,
     own_sem,
 ):
     F, B, T, TD, G, PX, rows, Uc, UB, RPF, nu, per = dims
@@ -104,6 +110,20 @@
     pix_u = lax.broadcasted_iota(jnp.int32, (1, rows), 1) + (corner_x + me * rows)
     pix_v = lax.broadcasted_iota(jnp.int32, (1, PX), 1) + corner_y
 
+    row = lax.broadcasted_iota(jnp.int32, meta_ref.shape, 0)
+    col = lax.broadcasted_iota(jnp.int32, meta_ref.shape, 1)
+    meta = jnp.where((col == 4) & (row < counts_ref[0]), 1, 0)
+    for t in range(TD):
+        for j in range(2):
+            meta = jnp.where((row == t) & (col == j), offsets_ref[t, j], meta)
+            meta = jnp.where((row == t) & (col == j + 2), stations_ref[t, j], meta)
+    meta_ref[...] = meta
+    for k in range(B):
+        c = lax.rem(me + k, B)
+        for j in range(nu):
+            u = c * Uc + (f // per) * nu + j
+            osend[c, j] = obs_ref[pl.ds(u, TD, stride=G), :]
+
     pl.semaphore_wait(barrier, B + F - 2)
 
     meta_copies = [zcopy(0, k, meta_ref, meta_land.at[me]) for k in range(1, B)]
@@ -111,8 +131,7 @@
     scr_copies = []
     for k in range(1, B):
         c = lax.rem(me + k, B)
-        u0 = c * Uc + (f // per) * nu
-        obs_copies.append(zcopy(1, k, obs_ref.at[pl.ds(u0, nu)], obs_land.at[me]))
+        obs_copies.append(zcopy(1, k, osend.at[c], obs_land.at[me]))
         scr_copies.append(
             zcopy(2, k, screens_ref.at[pl.ds(c * Uc, Uc)], scr_land.at[:, scr_rows(me)])
         )
@@ -124,7 +143,7 @@
     )
     own_copy.start()
     meta_land[me] = meta_ref[...]
-    obs_land[me] = obs_ref[pl.ds(me * Uc + (f // per) * nu, nu)]
+    obs_land[me] = osend[me]
 
     cells = lax.broadcasted_iota(jnp.int32, (G, 1), 0)
     cu, su = cis(cells * pix_u, N)
@@ -267,7 +286,7 @@
         copy.start()
     if per > 1:
         obsfull[...] = jnp.zeros_like(obsfull)
-    obsfull[span, :] = res
+    obsfull[span, :] = total
     for j in range(nu):
         for b in range(B):
             zsend[b, j] = obsfull[j * T + b * TD : j * T + (b + 1) * TD, :]
@@ -285,9 +304,31 @@
         return carry
 
     lax.fori_loop(0, Uc, weigh, 0)
-    w_copies = [zcopy(4, k, rall.at[me], rall.at[me]) for k in range(1, B)]
-    for copy in w_copies:
-        copy.start()
+
+    def right(n):
+        block = jnp.maximum(me - n, 0)
+        return pltpu.make_async_remote_copy(
+            src_ref=rall.at[block], dst_ref=rall.at[block],
+            send_sem=w_send.at[0, n], recv_sem=w_recv.at[0, n],
+            device_id={"bl": lax.rem(me + 1, B)}, device_id_type=pl.DeviceIdType.MESH,
+        )
+
+    def left_(n):
+        block = jnp.minimum(me + n, B - 1)
+        return pltpu.make_async_remote_copy(
+            src_ref=rall.at[block], dst_ref=rall.at[block],
+            send_sem=w_send.at[1, n], recv_sem=w_recv.at[1, n],
+            device_id={"bl": lax.rem(me + B - 1, B)}, device_id_type=pl.DeviceIdType.MESH,
+        )
+
+    def sends_right(n):
+        return (me - n >= 0) & (me + 1 < B)
+
+    def sends_left(n):
+        return (me + n < B) & (me >= 1)
+
+    pl.when(sends_right(0))(lambda: right(0).start())
+    pl.when(sends_left(0))(lambda: left_(0).start())
     z_copies = [
         zcopy(5, k, zsend.at[lax.rem(me + k, B)], reso.at[f, me]) for k in range(1, B)
     ]
@@ -322,13 +363,31 @@
     o_copies = [pcopy(2, k, reso.at[f], reso.at[f]) for k in range(1, F)]
     for copy in o_copies:
         copy.start()
-    for k in range(1, B):
-        w_copies[k - 1].wait()
-        image(lax.rem(me + B - k, B))
-    image_ref[...] = image_ref[...] * (1.0 / (32.0 * G * math.sqrt(T)))
+    for n in range(B - 1):
+        pl.when(me - 1 - n >= 0)(lambda n=n: right(n).wait_recv())
+        if n + 1 < B - 1:
+            pl.when(sends_right(n + 1))(lambda n=n: right(n + 1).start())
+        pl.when(me + 1 + n < B)(lambda n=n: left_(n).wait_recv())
+        if n + 1 < B - 1:
+            pl.when(sends_left(n + 1))(lambda n=n: left_(n + 1).start())
+
+        def arrived(side, carry, n=n):
+            src = jnp.where(side == 0, me - 1 - n, me + 1 + n)
+            pl.when((src >= 0) & (src < B))(lambda: image(src))
+            return carry
+
+        lax.fori_loop(0, 2, arrived, 0)
+    for n in range(B - 1):
+        pl.when(sends_right(n))(lambda n=n: right(n).wait_send())
+        pl.when(sends_left(n))(lambda n=n: left_(n).wait_send())
     for copy in o_copies:
         copy.wait()
-    resout_ref[...] = reso[...]
+    group = (me * TD) // RPF if per > 1 else 0
+    for g in range(F // per):
+        for c in range(B):
+            for j in range(nu):
+                u = c * Uc + g * nu + j
+                pred_ref[pl.ds(u, TD, stride=G), :] = reso[g * per + group, c, j]
 
 
 def per_device(F, B, facet_model, screens, observed, offsets, stations, counts):
@@ -344,23 +403,22 @@
     per = max(1, T // RPF)
     dims = (F, B, T, TD, G, PX, rows, Uc, UB, RPF, nu, per)
     tdp = -(-TD // 8) * 8
-    live = (jnp.arange(TD, dtype=jnp.int32) < counts[0]).astype(jnp.int32)[:, None]
-    meta = jnp.concatenate([offsets, stations, live], axis=1)
-    meta = jnp.pad(meta, ((0, tdp - TD), (0, 128 - meta.shape[1])))
     screens_t = jnp.transpose(screens[0], (1, 0, 2))
-    obs_t = jnp.transpose(observed, (1, 0, 2))
     W = 2 * G
     vmem = pl.BlockSpec(memory_space=pltpu.VMEM)
-    image, res = pl.pallas_call(
+    smem = pl.BlockSpec(memory_space=pltpu.SMEM)
+    image, predicted = pl.pallas_call(
         functools.partial(kernel, dims),
         out_shape=(
             jax.ShapeDtypeStruct((rows, PX), F32),
-            jax.ShapeDtypeStruct((F, B, nu, TD, W), F32),
+            jax.ShapeDtypeStruct((TD * G, W), F32),
         ),
-        in_specs=[vmem] * 4,
+        in_specs=[smem] * 3 + [vmem] * 3,
         out_specs=(vmem, vmem),
         scratch_shapes=[
+            pltpu.VMEM((tdp, 128), jnp.int32),
             pltpu.VMEM((B, tdp, 128), jnp.int32),
+            pltpu.VMEM((B, nu, TD, W), F32),
             pltpu.VMEM((T, 128), jnp.int32),
             pltpu.VMEM((2, G, rows), F32),
             pltpu.VMEM((2, T, rows), F32),
@@ -386,17 +444,17 @@
             pltpu.SemaphoreType.DMA((6, B)),
             pltpu.SemaphoreType.DMA((3, F)),
             pltpu.SemaphoreType.DMA((3, F)),
+            pltpu.SemaphoreType.DMA((2, B)),
+            pltpu.SemaphoreType.DMA((2, B)),
             pltpu.SemaphoreType.DMA,
         ],
         compiler_params=pltpu.CompilerParams(
             collective_id=0, has_side_effects=True, vmem_limit_bytes=56 * 1024 * 1024
         ),
-    )(meta, facet_model[0], screens_t, obs_t)
-    group = lax.axis_index("bl") * TD // RPF if per > 1 else 0
-    res = res.reshape(F // per, per, B, nu, TD, W)
-    res = lax.dynamic_index_in_dim(res, group, axis=1, keepdims=False)
-    res = jnp.transpose(res, (3, 1, 0, 2, 4)).reshape(TD, G, W)
-    return (res, image[None])
+    )(offsets, stations, counts, facet_model[0], screens_t, observed.reshape(TD * G, W))
+    live = (jnp.arange(TD, dtype=jnp.int32) < counts[0])[:, None, None]
+    residual = jnp.where(live, observed - predicted.reshape(TD, G, W), 0.0)
+    return (residual, image[None] * (1.0 / (32.0 * G * math.sqrt(T))))
 
 
 def solution(mesh):

time: 103 us -> 93.6 us (0.909)
  Pallas kernels: 90.3 us -> 84 us
  local copies, waits for them, and re-layouts: 11.2 us -> 4.93 us
  other arithmetic: 0.09 us -> 3.06 us
    pallas_call x1, Pallas kernels: 90.3 us -> 84 us  [per_device(): pl.pallas_call(functools.partial(kernel, dims), out_shape=(jax.ShapeDtype...]
    unnamed x9 -> x11, local copies, waits for them, and re-layouts: 8.64 us -> 4.93 us
    transpose x1 -> x0, local copies, waits for them, and re-layouts: 1.99 us -> none  [per_device(): res = jnp.transpose(res, (3, 1, 0, 2, 4)).reshape(TD, G, W)]
    select_n x0 -> x1, other arithmetic: none -> 1.94 us  [per_device(): residual = jnp.where(live, observed - predicted.reshape(TD, G, W), 0.0)]
    mul x0 -> x1, other arithmetic: none -> 1.12 us  [per_device(): return (residual, image[None] * (1.0 / (32.0 * G * math.sqrt(T))))]
where the time goes in v2:
time: 93.6 us; the launch traced here: 93.3 us
  Pallas kernels  84 us (90%)
  local copies, waits for them, and re-layouts  4.93 us (5%)
  other arithmetic  3.06 us (3%)
  between operations  1.31 us (1%)
    pallas_call x1, Pallas kernels, per_device(): pl.pallas_call(functools.partial(kernel, dims), out_shape=(jax.ShapeDtype...  84 us
    unnamed x11, local copies, waits for them, and re-layouts  4.93 us
    select_n x1, other arithmetic, per_device(): residual = jnp.where(live, observed - predicted.reshape(TD, G, W), 0.0)  1.94 us

profile of v2, /device:TPU:0, one launch (start us, length us, event | category | flops | bytes accessed | tf_op | source)
XLA Modules:
  0.0 93.3 jit_solution(11850227142732420542)
XLA Ops:
  1.3 2.9 %copy.12 = bf16[1,64,64,128]{3,1,2,0:T(8,128)(2,1)} copy(bf16[1,64,64,128]{3,2,1,0:T(8,128)(2,1)} %param.7) | data formatting | bytes 2097152 | tf_op args[1]
  4.2 0.0 copy-start.2
  4.2 0.7 copy-done.2
  4.8 0.0 copy-start.3
  4.8 0.7 copy.10.stations_ref
  5.5 0.0 copy-done.3
  5.5 0.7 copy.9.offsets_ref
  6.2 0.0 copy-start
  6.2 84.0 %shard_map.77 = (f32[256,1024]{1,0:T(8,128)}, f32[768,128]{1,0:T(8,128)}) custom-call(s32[12,2]{1,0:T(8,128)} %copy.9.offsets_ref, s32[12,2]{1,0:T(8,128)} %copy.10.stations_ref, s32[1]{0:T(128)} %copy.13.counts_ref, bf16[256,1024]{1,0:T(8,128)(2,1)} %bitcast.14, bf16[64,64,128]{2,1,0:T(8,128)(2,1)} %bitcast.12, f32[768,128]{1,0:T(8,128)} %bitcast.13), custom_call_target="tpu_custom_call" | custom-call | tf_op jit(solution)/shard_map/pallas_call | solution.py:410
  90.2 0.0 copy-start.1
  90.2 0.0 copy-done
  90.2 1.9 %subtract_select_fusion = f32[12,64,128]{2,1,0:T(8,128)} fusion(f32[12,64,128]{2,1,0:T(8,128)S(1)} %copy-done, f32[12,64,128]{2,1,0:T(8,128)} %bitcast.15, pred[12]{0:T(512)(128)(4,1)S(1)} %iota_compare_fusion), kind=kLoop, calls=%fused_computation.2 | loop fusion | flops 196608 | bytes 1179660 | tf_op jit(solution)/shard_map/jit(_where)/select_n | solution.py:456
  92.2 0.0 copy-done.1
  92.2 1.1 %multiply_bitcast_fusion = f32[1,256,1024]{2,1,0:T(8,128)} fusion(f32[256,1024]{1,0:T(8,128)S(1)} %copy-done.1), kind=kLoop, calls=%fused_computation.1 | loop fusion | flops 262144 | bytes 2097152 | tf_op jit(solution)/shard_map/mul | solution.py:457
  (1 shorter events, 0.0 us)
Async XLA Ops:
  4.2 0.7 copy-start.2
  4.8 0.7 copy-start.3
  6.2 84.0 %copy-start = (f32[12,64,128]{2,1,0:T(8,128)S(1)}, f32[12,64,128]{2,1,0:T(8,128)}, u32[]{:S(2)}) copy-start(f32[12,64,128]{2,1,0:T(8,128)} %param.8) | copy-start | bytes 1179652
  90.2 2.0 %copy-start.1 = (f32[256,1024]{1,0:T(8,128)S(1)}, f32[256,1024]{1,0:T(8,128)}, u32[]{:S(2)}) copy-start(f32[256,1024]{1,0:T(8,128)} %get-tuple-element.5) | copy-start | bytes 3145732

commit v3 on v2

--- a/solution.py
+++ b/solution.py
@@ -47,6 +47,7 @@
     e1v,
     wv,
     tabu,
+    scr_raw,
     scr_land,
     sbuf,
     s_land,
@@ -68,13 +69,16 @@
     p_recv,
     w_send,
     w_recv,
+    s_send,
+    s_recv,
     own_sem,
 ):
     F, B, T, TD, G, PX, rows, Uc, UB, RPF, nu, per = dims
     N = FGRID * PX
     f = lax.axis_index("facet")
     me = lax.axis_index("bl")
-    spd = screens_ref.shape[1]
+    raw = Uc % 16 == 0
+    spd = screens_ref.shape[0 if raw else 1]
     UBT = UB * T
     H = G
 
@@ -115,8 +119,8 @@
     meta = jnp.where((col == 4) & (row < counts_ref[0]), 1, 0)
     for t in range(TD):
         for j in range(2):
-            meta = jnp.where((row == t) & (col == j), offsets_ref[t, j], meta)
-            meta = jnp.where((row == t) & (col == j + 2), stations_ref[t, j], meta)
+            meta = jnp.where((row == t) & (col == j), offsets_ref[j, t], meta)
+            meta = jnp.where((row == t) & (col == j + 2), stations_ref[j, t], meta)
     meta_ref[...] = meta
     for k in range(B):
         c = lax.rem(me + k, B)
@@ -132,15 +136,24 @@
     for k in range(1, B):
         c = lax.rem(me + k, B)
         obs_copies.append(zcopy(1, k, osend.at[c], obs_land.at[me]))
-        scr_copies.append(
-            zcopy(2, k, screens_ref.at[pl.ds(c * Uc, Uc)], scr_land.at[:, scr_rows(me)])
-        )
-    for group in (meta_copies, obs_copies, scr_copies):
+        if raw:
+            rows_c = pl.ds(pl.multiple_of(c * Uc, Uc), Uc)
+            scr_copies.append(zcopy(2, k, screens_ref.at[:, rows_c], scr_raw.at[me]))
+        else:
+            scr_copies.append(
+                zcopy(2, k, screens_ref.at[pl.ds(c * Uc, Uc)], scr_land.at[:, scr_rows(me)])
+            )
+    for group in (meta_copies, obs_copies, scr_copies[0::2]):
         for copy in group:
             copy.start()
-    own_copy = pltpu.make_async_copy(
-        screens_ref.at[pl.ds(me * Uc, Uc)], scr_land.at[:, scr_rows(me)], own_sem
-    )
+    if raw:
+        own_copy = pltpu.make_async_copy(
+            screens_ref.at[:, pl.ds(pl.multiple_of(me * Uc, Uc), Uc)], scr_raw.at[me], own_sem
+        )
+    else:
+        own_copy = pltpu.make_async_copy(
+            screens_ref.at[pl.ds(me * Uc, Uc)], scr_land.at[:, scr_rows(me)], own_sem
+        )
     own_copy.start()
     meta_land[me] = meta_ref[...]
     obs_land[me] = osend[me]
@@ -200,26 +213,49 @@
         )
         return b[:UBT] * sgn + swap(b[UBT:])
 
-    s_copies = []
-    for k in range(1, B):
-        c = lax.rem(me + k, B)
-
-        def body(i, carry, c=c):
+    def chain(side, d):
+        to = lax.rem(me + 1, B) if side == 0 else lax.rem(me + B - 1, B)
+        return pltpu.make_async_remote_copy(
+            src_ref=sbuf.at[d], dst_ref=s_land.at[side, d],
+            send_sem=s_send.at[side, d], recv_sem=s_recv.at[side, d],
+            device_id={"bl": to}, device_id_type=pl.DeviceIdType.MESH,
+        )
+
+    def passes(side, d):
+        return me < d if side == 0 else me > d
+
+    def first(side):
+        return me == 0 if side == 0 else me == B - 1
+
+    order = []
+    for n in range(B):
+        for d in (B - 1 - n, n):
+            if d not in order:
+                order.append(d)
+    for d in order:
+
+        def body(i, carry, d=d):
             rows_i = pl.ds(pl.multiple_of(i * UBT, UBT), UBT)
-            sbuf[c, rows_i, :] = predict(c, i).astype(BF16)
+            sbuf[d, rows_i, :] = predict(d, i).astype(BF16)
             return carry
 
         lax.fori_loop(0, nchunk, body, 0)
-        copy = zcopy(3, k, sbuf.at[c], s_land.at[me])
-        copy.start()
-        s_copies.append(copy)
-
-    def body_own(i, carry):
-        rows_i = pl.ds(pl.multiple_of(i * UBT, UBT), UBT)
-        sown[rows_i, :] = predict(me, i)
-        return carry
-
-    lax.fori_loop(0, nchunk, body_own, 0)
+        for side in range(2):
+            pl.when(first(side) & passes(side, d))(lambda: chain(side, d).start())
+
+    def pass_on(side, d):
+        @pl.when(jnp.logical_not(first(side)) & passes(side, d))
+        def _():
+            chain(side, d).wait_recv()
+            sbuf[d] = (sbuf[d].astype(F32) + s_land[side, d].astype(F32)).astype(BF16)
+            chain(side, d).start()
+
+    for n in range(B - 1):
+        pass_on(0, B - 1 - n)
+        pass_on(1, n)
+        if n == 0:
+            for copy in scr_copies[1::2]:
+                copy.start()
 
     for copy in obs_copies:
         copy.wait()
@@ -233,6 +269,10 @@
     own_copy.wait()
     for copy in scr_copies:
         copy.wait()
+    if raw:
+        for b in range(B):
+            block = jnp.swapaxes(scr_raw[b].astype(F32), 0, 1)
+            scr_land[:, b * spd : (b + 1) * spd, :] = block.astype(BF16)
     stations = lax.broadcasted_iota(jnp.int32, (1, B * spd), 1)
     pick = jnp.concatenate([meta_all[:, 2:3], meta_all[:, 3:4]], axis=0) == stations
     pick = jnp.where(pick, 1.0, 0.0).astype(BF16)
@@ -248,14 +288,17 @@
 
     lax.fori_loop(0, Uc, gains, 0)
 
-    for copy in s_copies:
-        copy.wait()
+    sown[...] = sbuf[me].astype(F32)
+    for side in range(2):
+
+        @pl.when(jnp.logical_not(first(side)))
+        def _(side=side):
+            chain(side, me).wait_recv()
+            sown[...] += s_land[side, me].astype(F32)
 
     def contribution(u, carry):
         r = pl.ds(pl.multiple_of(u * T, T), T)
         s = sown[r, :]
-        for k in range(1, B):
-            s = s + s_land[lax.rem(me + k, B), r, :].astype(F32)
         g = gbuf[r, :]
         gsw = swap(g)
         out = s * jnp.where(left, g, gsw) + swap(s) * jnp.where(left, -gsw, g)
@@ -380,6 +423,9 @@
     for n in range(B - 1):
         pl.when(sends_right(n))(lambda n=n: right(n).wait_send())
         pl.when(sends_left(n))(lambda n=n: left_(n).wait_send())
+    for d in range(B):
+        for side in range(2):
+            pl.when(passes(side, d))(lambda: chain(side, d).wait_send())
     for copy in o_copies:
         copy.wait()
     group = (me * TD) // RPF if per > 1 else 0
@@ -397,13 +443,14 @@
     spd = screens.shape[1]
     T = TD * B
     Uc = G // B
-    UB = max(1, min(Uc, 192 // T))
+    UB = max(1, min(Uc, 384 // T))
     RPF = Uc * T // F
     nu = max(1, RPF // T)
     per = max(1, T // RPF)
     dims = (F, B, T, TD, G, PX, rows, Uc, UB, RPF, nu, per)
     tdp = -(-TD // 8) * 8
-    screens_t = jnp.transpose(screens[0], (1, 0, 2))
+    raw = Uc % 16 == 0
+    gains = screens[0] if raw else jnp.transpose(screens[0], (1, 0, 2))
     W = 2 * G
     vmem = pl.BlockSpec(memory_space=pltpu.VMEM)
     smem = pl.BlockSpec(memory_space=pltpu.SMEM)
@@ -425,9 +472,10 @@
             pltpu.VMEM((2, T, PX), F32),
             pltpu.VMEM((W, PX), BF16),
             pltpu.VMEM((G // UB, 2 * UB * T, rows), BF16),
+            pltpu.VMEM((B, spd, Uc, W) if raw else (1, 16, 128), BF16),
             pltpu.VMEM((Uc, B * spd, W), BF16),
             pltpu.VMEM((B, Uc * T, W), BF16),
-            pltpu.VMEM((B, Uc * T, W), BF16),
+            pltpu.VMEM((2, B, Uc * T, W), BF16),
             pltpu.VMEM((Uc * T, W), F32),
             pltpu.VMEM((Uc * T, W), F32),
             pltpu.VMEM((Uc * T, W), BF16),
@@ -446,12 +494,14 @@
             pltpu.SemaphoreType.DMA((3, F)),
             pltpu.SemaphoreType.DMA((2, B)),
             pltpu.SemaphoreType.DMA((2, B)),
+            pltpu.SemaphoreType.DMA((2, B)),
+            pltpu.SemaphoreType.DMA((2, B)),
             pltpu.SemaphoreType.DMA,
         ],
         compiler_params=pltpu.CompilerParams(
             collective_id=0, has_side_effects=True, vmem_limit_bytes=56 * 1024 * 1024
         ),
-    )(offsets, stations, counts, facet_model[0], screens_t, observed.reshape(TD * G, W))
+    )(offsets.T, stations.T, counts, facet_model[0], gains, observed.reshape(TD * G, W))
     live = (jnp.arange(TD, dtype=jnp.int32) < counts[0])[:, None, None]
     residual = jnp.where(live, observed - predicted.reshape(TD, G, W), 0.0)
     return (residual, image[None] * (1.0 / (32.0 * G * math.sqrt(T))))

time: 93.6 us -> 91.5 us (0.978)
  local copies, waits for them, and re-layouts: 4.93 us -> 0.01 us
  Pallas kernels: 84 us -> 87 us
    unnamed x11 -> x4, local copies, waits for them, and re-layouts: 4.93 us -> 0.01 us
    pallas_call x1, Pallas kernels: 84 us -> 87 us  [per_device(): pl.pallas_call(functools.partial(kernel, dims), out_shape=(jax.ShapeDtype...]
where the time goes in v3:
time: 91.5 us; the launch traced here: 91.4 us
  Pallas kernels  87 us (95%)
  other arithmetic  3.07 us (3%)
  between operations  1.32 us (1%)
    pallas_call x1, Pallas kernels, per_device(): pl.pallas_call(functools.partial(kernel, dims), out_shape=(jax.ShapeDtype...  87 us
    select_n x1, other arithmetic, per_device(): residual = jnp.where(live, observed - predicted.reshape(TD, G, W), 0.0)  1.94 us

profile of v3, /device:TPU:0, one launch (start us, length us, event | category | flops | bytes accessed | tf_op | source)
XLA Modules:
  0.0 91.4 jit_solution(12380085937729361533)
XLA Ops:
  1.3 0.0 copy-start
  1.3 87.0 %shard_map.77 = (f32[256,1024]{1,0:T(8,128)}, f32[768,128]{1,0:T(8,128)}) custom-call(s32[2,12]{1,0:T(2,128)} %bitcast.14, s32[2,12]{1,0:T(2,128)} %bitcast.15, s32[1]{0:T(128)} %copy.8.counts_ref, bf16[256,1024]{1,0:T(8,128)(2,1)} %bitcast.12, bf16[64,64,128]{2,1,0:T(8,128)(2,1)} %bitcast.11, f32[768,128]{1,0:T(8,128)} %bitcast.10), custom_call_target="tpu_custom_call" | custom-call | tf_op jit(solution)/shard_map/pallas_call | solution.py:457
  88.3 0.0 copy-start.1
  88.3 0.0 copy-done
  88.3 1.9 %subtract_select_fusion = f32[12,64,128]{2,1,0:T(8,128)} fusion(f32[12,64,128]{2,1,0:T(8,128)S(1)} %copy-done, f32[12,64,128]{2,1,0:T(8,128)} %bitcast.13, pred[12]{0:T(512)(128)(4,1)S(1)} %iota_compare_fusion), kind=kLoop, calls=%fused_computation.1 | loop fusion | flops 196608 | bytes 1179660 | tf_op jit(solution)/shard_map/jit(_where)/select_n | solution.py:506
  90.2 0.0 copy-done.1
  90.2 1.1 %multiply_bitcast_fusion = f32[1,256,1024]{2,1,0:T(8,128)} fusion(f32[256,1024]{1,0:T(8,128)S(1)} %copy-done.1), kind=kLoop, calls=%fused_computation | loop fusion | flops 262144 | bytes 2097152 | tf_op jit(solution)/shard_map/mul | solution.py:507
  (1 shorter events, 0.0 us)
Async XLA Ops:
  1.3 87.0 %copy-start = (f32[12,64,128]{2,1,0:T(8,128)S(1)}, f32[12,64,128]{2,1,0:T(8,128)}, u32[]{:S(2)}) copy-start(f32[12,64,128]{2,1,0:T(8,128)} %param.8) | copy-start | bytes 1179652
  88.3 2.0 %copy-start.1 = (f32[256,1024]{1,0:T(8,128)S(1)}, f32[256,1024]{1,0:T(8,128)}, u32[]{:S(2)}) copy-start(f32[256,1024]{1,0:T(8,128)} %get-tuple-element.5) | copy-start | bytes 3145732

commit v4 on v3

--- a/solution.py
+++ b/solution.py
@@ -45,8 +45,11 @@
     e2u,
     e1u,
     e1v,
+    e2v,
     wv,
+    tabv,
     tabu,
+    s32,
     scr_raw,
     scr_land,
     sbuf,
@@ -73,13 +76,14 @@
     s_recv,
     own_sem,
 ):
-    F, B, T, TD, G, PX, rows, Uc, UB, RPF, nu, per = dims
+    F, B, T, TD, G, PX, rows, Uc, UB, NT, RPF, nu, per = dims
     N = FGRID * PX
     f = lax.axis_index("facet")
     me = lax.axis_index("bl")
     raw = Uc % 16 == 0
     spd = screens_ref.shape[0 if raw else 1]
     UBT = UB * T
+    W = 2 * G
     H = G
 
     barrier = pltpu.get_barrier_semaphore()
@@ -164,6 +168,8 @@
     e2u[1] = su
     for j in range(0, PX, 256):
         cv, sv = cis(cells * pix_v[:, j : j + 256], N)
+        e2v[0, :, j : j + 256] = cv
+        e2v[1, :, j : j + 256] = sv
         wv[:H, j : j + 256] = cv.astype(BF16)
         wv[H:, j : j + 256] = sv.astype(BF16)
 
@@ -190,28 +196,41 @@
 
     nchunk = Uc // UB
 
-    def predict(c, i):
-        ci = c * nchunk + i
+    def predict(g, carry):
+        for j in range(NT):
+            t = g * NT + j
+            a_c = e1v[0, pl.ds(t, 1), :]
+            a_s = e1v[1, pl.ds(t, 1), :]
+            tabv[j * W : j * W + H, :] = (a_c * e2v[0] - a_s * e2v[1]).astype(BF16)
+            tabv[j * W + H : (j + 1) * W, :] = (a_s * e2v[0] + a_c * e2v[1]).astype(BF16)
+        x = lax.dot_general(
+            tabv[...], model_ref[...], (((1,), (1,)), ((), ())), preferred_element_type=F32
+        ).astype(BF16)
+        for j in range(NT):
+            t = g * NT + j
+            a_c = e1u[0, pl.ds(t, 1), :]
+            a_s = e1u[1, pl.ds(t, 1), :]
+            top = (a_c * e2u[0] - a_s * e2u[1]).astype(BF16)
+            bot = (-(a_s * e2u[0] + a_c * e2u[1])).astype(BF16)
+            b = lax.dot_general(
+                jnp.concatenate([top, bot], axis=0), x[j * W : (j + 1) * W],
+                (((1,), (1,)), ((), ())), preferred_element_type=F32,
+            )
+            s32[pl.ds(t, G, stride=T), :] = b[:H] * sgn + swap(b[H:])
+        return carry
+
+    lax.fori_loop(0, T // NT, predict, 0)
+
+    def image_table(ci, carry):
         for j in range(UB):
-            u = c * Uc + i * UB + j
+            u = ci * UB + j
             e2c = e2u[0, pl.ds(u, 1), :]
             e2s = e2u[1, pl.ds(u, 1), :]
             a_c = e1u[0]
             a_s = e1u[1]
             tabu[ci, j * T : (j + 1) * T, :] = (a_c * e2c - a_s * e2s).astype(BF16)
             tabu[ci, UBT + j * T : UBT + (j + 1) * T, :] = (-(a_s * e2c + a_c * e2s)).astype(BF16)
-        up = jnp.dot(tabu[ci], model_ref[...], preferred_element_type=F32)
-        tops, bots = [], []
-        for j in range(UB):
-            uc = up[j * T : (j + 1) * T]
-            us = up[UBT + j * T : UBT + (j + 1) * T]
-            tops.append((uc * e1v[0] + us * e1v[1]).astype(BF16))
-            bots.append((us * e1v[0] - uc * e1v[1]).astype(BF16))
-        both = jnp.concatenate(tops + bots, axis=0)
-        b = lax.dot_general(
-            both, wv[...], (((1,), (1,)), ((), ())), preferred_element_type=F32
-        )
-        return b[:UBT] * sgn + swap(b[UBT:])
+        return carry
 
     def chain(side, d):
         to = lax.rem(me + 1, B) if side == 0 else lax.rem(me + B - 1, B)
@@ -233,13 +252,7 @@
             if d not in order:
                 order.append(d)
     for d in order:
-
-        def body(i, carry, d=d):
-            rows_i = pl.ds(pl.multiple_of(i * UBT, UBT), UBT)
-            sbuf[d, rows_i, :] = predict(d, i).astype(BF16)
-            return carry
-
-        lax.fori_loop(0, nchunk, body, 0)
+        sbuf[d] = s32[d * Uc * T : (d + 1) * Uc * T, :].astype(BF16)
         for side in range(2):
             pl.when(first(side) & passes(side, d))(lambda: chain(side, d).start())
 
@@ -315,6 +328,7 @@
     ]
     for copy in c_copies:
         copy.start()
+    lax.fori_loop(0, G // UB, image_table, 0)
     total = cbuf[piece(f), :].astype(F32)
     for copy in c_copies:
         copy.wait()
@@ -444,10 +458,11 @@
     T = TD * B
     Uc = G // B
     UB = max(1, min(Uc, 384 // T))
+    NT = 4 if T % 4 == 0 else 1
     RPF = Uc * T // F
     nu = max(1, RPF // T)
     per = max(1, T // RPF)
-    dims = (F, B, T, TD, G, PX, rows, Uc, UB, RPF, nu, per)
+    dims = (F, B, T, TD, G, PX, rows, Uc, UB, NT, RPF, nu, per)
     tdp = -(-TD // 8) * 8
     raw = Uc % 16 == 0
     gains = screens[0] if raw else jnp.transpose(screens[0], (1, 0, 2))
@@ -470,8 +485,11 @@
             pltpu.VMEM((2, G, rows), F32),
             pltpu.VMEM((2, T, rows), F32),
             pltpu.VMEM((2, T, PX), F32),
+            pltpu.VMEM((2, G, PX), F32),
             pltpu.VMEM((W, PX), BF16),
+            pltpu.VMEM((NT * W, PX), BF16),
             pltpu.VMEM((G // UB, 2 * UB * T, rows), BF16),
+            pltpu.VMEM((G * T, W), F32),
             pltpu.VMEM((B, spd, Uc, W) if raw else (1, 16, 128), BF16),
             pltpu.VMEM((Uc, B * spd, W), BF16),
             pltpu.VMEM((B, Uc * T, W), BF16),

time: 91.5 us -> 91.8 us (level)
  no operation moved by 1% of the time
where the time goes in v4:
time: 91.8 us; the launch traced here: 91.7 us
  Pallas kernels  87.3 us (95%)
  other arithmetic  3.07 us (3%)
  between operations  1.32 us (1%)
    pallas_call x1, Pallas kernels, per_device(): pl.pallas_call(functools.partial(kernel, dims), out_shape=(jax.ShapeDtype...  87.3 us
    select_n x1, other arithmetic, per_device(): residual = jnp.where(live, observed - predicted.reshape(TD, G, W), 0.0)  1.94 us

profile of v4, /device:TPU:0, one launch (start us, length us, event | category | flops | bytes accessed | tf_op | source)
XLA Modules:
  0.0 91.7 jit_solution(11165832918207434692)
XLA Ops:
  1.3 0.0 copy-start
  1.3 87.3 %shard_map.77 = (f32[256,1024]{1,0:T(8,128)}, f32[768,128]{1,0:T(8,128)}) custom-call(s32[2,12]{1,0:T(2,128)} %bitcast.14, s32[2,12]{1,0:T(2,128)} %bitcast.15, s32[1]{0:T(128)} %copy.8.counts_ref, bf16[256,1024]{1,0:T(8,128)(2,1)} %bitcast.12, bf16[64,64,128]{2,1,0:T(8,128)(2,1)} %bitcast.11, f32[768,128]{1,0:T(8,128)} %bitcast.10), custom_call_target="tpu_custom_call" | custom-call | tf_op jit(solution)/shard_map/pallas_call | solution.py:472
  88.6 0.0 copy-start.1
  88.6 0.0 copy-done
  88.6 1.9 %subtract_select_fusion = f32[12,64,128]{2,1,0:T(8,128)} fusion(f32[12,64,128]{2,1,0:T(8,128)S(1)} %copy-done, f32[12,64,128]{2,1,0:T(8,128)} %bitcast.13, pred[12]{0:T(512)(128)(4,1)S(1)} %iota_compare_fusion), kind=kLoop, calls=%fused_computation.1 | loop fusion | flops 196608 | bytes 1179660 | tf_op jit(solution)/shard_map/jit(_where)/select_n | solution.py:524
  90.6 0.0 copy-done.1
  90.6 1.1 %multiply_bitcast_fusion = f32[1,256,1024]{2,1,0:T(8,128)} fusion(f32[256,1024]{1,0:T(8,128)S(1)} %copy-done.1), kind=kLoop, calls=%fused_computation | loop fusion | flops 262144 | bytes 2097152 | tf_op jit(solution)/shard_map/mul | solution.py:525
  (1 shorter events, 0.0 us)
Async XLA Ops:
  1.3 87.3 %copy-start = (f32[12,64,128]{2,1,0:T(8,128)S(1)}, f32[12,64,128]{2,1,0:T(8,128)}, u32[]{:S(2)}) copy-start(f32[12,64,128]{2,1,0:T(8,128)} %param.8) | copy-start | bytes 1179652
  88.6 2.0 %copy-start.1 = (f32[256,1024]{1,0:T(8,128)S(1)}, f32[256,1024]{1,0:T(8,128)}, u32[]{:S(2)}) copy-start(f32[256,1024]{1,0:T(8,128)} %get-tuple-element.5) | copy-start | bytes 3145732

commit v5 on v4

--- a/solution.py
+++ b/solution.py
@@ -263,12 +263,24 @@
             sbuf[d] = (sbuf[d].astype(F32) + s_land[side, d].astype(F32)).astype(BF16)
             chain(side, d).start()
 
+    for copy in scr_copies[1::2]:
+        copy.start()
+
+    def stand(b):
+        if raw:
+            block = jnp.swapaxes(scr_raw[b].astype(F32), 0, 1)
+            scr_land[:, scr_rows(b), :] = block.astype(BF16)
+
+    own_copy.wait()
+    stand(me)
+    early = list(range(1, B, 2))
     for n in range(B - 1):
         pass_on(0, B - 1 - n)
         pass_on(1, n)
-        if n == 0:
-            for copy in scr_copies[1::2]:
-                copy.start()
+        if early:
+            k = early.pop(0)
+            scr_copies[k - 1].wait()
+            stand(lax.rem(me + B - k, B))
 
     for copy in obs_copies:
         copy.wait()
@@ -279,13 +291,9 @@
             meta_all[:, 4:5].astype(F32), (T, 2 * G)
         )
 
-    own_copy.wait()
-    for copy in scr_copies:
-        copy.wait()
-    if raw:
-        for b in range(B):
-            block = jnp.swapaxes(scr_raw[b].astype(F32), 0, 1)
-            scr_land[:, b * spd : (b + 1) * spd, :] = block.astype(BF16)
+    for k in range(2, B, 2):
+        scr_copies[k - 1].wait()
+        stand(lax.rem(me + B - k, B))
     stations = lax.broadcasted_iota(jnp.int32, (1, B * spd), 1)
     pick = jnp.concatenate([meta_all[:, 2:3], meta_all[:, 3:4]], axis=0) == stations
     pick = jnp.where(pick, 1.0, 0.0).astype(BF16)
@@ -299,7 +307,7 @@
         gbuf[pl.ds(pl.multiple_of(u * T, T), T), :] = g
         return carry
 
-    lax.fori_loop(0, Uc, gains, 0)
+    lax.fori_loop(0, Uc, gains, 0, unroll=4)
 
     sown[...] = sbuf[me].astype(F32)
     for side in range(2):
@@ -318,7 +326,7 @@
         cbuf[r, :] = out.astype(BF16)
         return carry
 
-    lax.fori_loop(0, Uc, contribution, 0)
+    lax.fori_loop(0, Uc, contribution, 0, unroll=4)
 
     def piece(i):
         return pl.ds(pl.multiple_of(i * RPF, RPF), RPF)
@@ -360,7 +368,7 @@
         rall[me, r, :] = out.astype(BF16)
         return carry
 
-    lax.fori_loop(0, Uc, weigh, 0)
+    lax.fori_loop(0, Uc, weigh, 0, unroll=4)
 
     def right(n):
         block = jnp.maximum(me - n, 0)

time: 91.8 us -> 85 us (0.926)
  Pallas kernels: 87.3 us -> 80.4 us
    pallas_call x1, Pallas kernels: 87.3 us -> 80.4 us  [per_device(): pl.pallas_call(functools.partial(kernel, dims), out_shape=(jax.ShapeDtype...]
where the time goes in v5:
time: 85 us; the launch traced here: 84.8 us
  Pallas kernels  80.4 us (95%)
  other arithmetic  3.07 us (4%)
  between operations  1.32 us (2%)
    pallas_call x1, Pallas kernels, per_device(): pl.pallas_call(functools.partial(kernel, dims), out_shape=(jax.ShapeDtype...  80.4 us
    select_n x1, other arithmetic, per_device(): residual = jnp.where(live, observed - predicted.reshape(TD, G, W), 0.0)  1.94 us

profile of v5, /device:TPU:0, one launch (start us, length us, event | category | flops | bytes accessed | tf_op | source)
XLA Modules:
  0.0 84.8 jit_solution(5599342719897634440)
XLA Ops:
  1.3 0.0 copy-start
  1.3 80.4 %shard_map.77 = (f32[256,1024]{1,0:T(8,128)}, f32[768,128]{1,0:T(8,128)}) custom-call(s32[2,12]{1,0:T(2,128)} %bitcast.14, s32[2,12]{1,0:T(2,128)} %bitcast.15, s32[1]{0:T(128)} %copy.8.counts_ref, bf16[256,1024]{1,0:T(8,128)(2,1)} %bitcast.12, bf16[64,64,128]{2,1,0:T(8,128)(2,1)} %bitcast.11, f32[768,128]{1,0:T(8,128)} %bitcast.10), custom_call_target="tpu_custom_call" | custom-call | tf_op jit(solution)/shard_map/pallas_call | solution.py:480
  81.7 0.0 copy-start.1
  81.7 0.0 copy-done
  81.7 1.9 %subtract_select_fusion = f32[12,64,128]{2,1,0:T(8,128)} fusion(f32[12,64,128]{2,1,0:T(8,128)S(1)} %copy-done, f32[12,64,128]{2,1,0:T(8,128)} %bitcast.13, pred[12]{0:T(512)(128)(4,1)S(1)} %iota_compare_fusion), kind=kLoop, calls=%fused_computation.1 | loop fusion | flops 196608 | bytes 1179660 | tf_op jit(solution)/shard_map/jit(_where)/select_n | solution.py:532
  83.7 0.0 copy-done.1
  83.7 1.1 %multiply_bitcast_fusion = f32[1,256,1024]{2,1,0:T(8,128)} fusion(f32[256,1024]{1,0:T(8,128)S(1)} %copy-done.1), kind=kLoop, calls=%fused_computation | loop fusion | flops 262144 | bytes 2097152 | tf_op jit(solution)/shard_map/mul | solution.py:533
  (1 shorter events, 0.0 us)
Async XLA Ops:
  1.3 80.4 %copy-start = (f32[12,64,128]{2,1,0:T(8,128)S(1)}, f32[12,64,128]{2,1,0:T(8,128)}, u32[]{:S(2)}) copy-start(f32[12,64,128]{2,1,0:T(8,128)} %param.8) | copy-start | bytes 1179652
  81.7 2.0 %copy-start.1 = (f32[256,1024]{1,0:T(8,128)S(1)}, f32[256,1024]{1,0:T(8,128)}, u32[]{:S(2)}) copy-start(f32[256,1024]{1,0:T(8,128)} %get-tuple-element.5) | copy-start | bytes 3145732

commit v6 on v5

--- a/solution.py
+++ b/solution.py
@@ -147,7 +147,7 @@
             scr_copies.append(
                 zcopy(2, k, screens_ref.at[pl.ds(c * Uc, Uc)], scr_land.at[:, scr_rows(me)])
             )
-    for group in (meta_copies, obs_copies, scr_copies[0::2]):
+    for group in (meta_copies, obs_copies, scr_copies[0::2], scr_copies[1::2]):
         for copy in group:
             copy.start()
     if raw:
@@ -262,9 +262,6 @@
             chain(side, d).wait_recv()
             sbuf[d] = (sbuf[d].astype(F32) + s_land[side, d].astype(F32)).astype(BF16)
             chain(side, d).start()
-
-    for copy in scr_copies[1::2]:
-        copy.start()
 
     def stand(b):
         if raw:
@@ -429,6 +426,15 @@
     for copy in o_copies:
         copy.start()
     for n in range(B - 1):
+        if n == B - 2:
+            for copy in o_copies:
+                copy.wait()
+            group = (me * TD) // RPF if per > 1 else 0
+            for g in range(F // per):
+                for c in range(B):
+                    for j in range(nu):
+                        u = c * Uc + g * nu + j
+                        pred_ref[pl.ds(u, TD, stride=G), :] = reso[g * per + group, c, j]
         pl.when(me - 1 - n >= 0)(lambda n=n: right(n).wait_recv())
         if n + 1 < B - 1:
             pl.when(sends_right(n + 1))(lambda n=n: right(n + 1).start())
@@ -448,14 +454,6 @@
     for d in range(B):
         for side in range(2):
             pl.when(passes(side, d))(lambda: chain(side, d).wait_send())
-    for copy in o_copies:
-        copy.wait()
-    group = (me * TD) // RPF if per > 1 else 0
-    for g in range(F // per):
-        for c in range(B):
-            for j in range(nu):
-                u = c * Uc + g * nu + j
-                pred_ref[pl.ds(u, TD, stride=G), :] = reso[g * per + group, c, j]
 
 
 def per_device(F, B, facet_model, screens, observed, offsets, stations, counts):

time: 85 us -> 83.8 us (0.986)
  Pallas kernels: 80.4 us -> 79.2 us
    pallas_call x1, Pallas kernels: 80.4 us -> 79.2 us  [per_device(): pl.pallas_call(functools.partial(kernel, dims), out_shape=(jax.ShapeDtype...]
where the time goes in v6:
time: 83.8 us; the launch traced here: 83.6 us
  Pallas kernels  79.2 us (95%)
  other arithmetic  3.07 us (4%)
  between operations  1.32 us (2%)
    pallas_call x1, Pallas kernels, per_device(): pl.pallas_call(functools.partial(kernel, dims), out_shape=(jax.ShapeDtype...  79.2 us
    select_n x1, other arithmetic, per_device(): residual = jnp.where(live, observed - predicted.reshape(TD, G, W), 0.0)  1.94 us

profile of v6, /device:TPU:0, one launch (start us, length us, event | category | flops | bytes accessed | tf_op | source)
XLA Modules:
  0.0 83.6 jit_solution(1322023589749106453)
XLA Ops:
  1.3 0.0 copy-start
  1.3 79.2 %shard_map.77 = (f32[256,1024]{1,0:T(8,128)}, f32[768,128]{1,0:T(8,128)}) custom-call(s32[2,12]{1,0:T(2,128)} %bitcast.14, s32[2,12]{1,0:T(2,128)} %bitcast.15, s32[1]{0:T(128)} %copy.8.counts_ref, bf16[256,1024]{1,0:T(8,128)(2,1)} %bitcast.12, bf16[64,64,128]{2,1,0:T(8,128)(2,1)} %bitcast.11, f32[768,128]{1,0:T(8,128)} %bitcast.10), custom_call_target="tpu_custom_call" | custom-call | tf_op jit(solution)/shard_map/pallas_call | solution.py:478
  80.6 0.0 copy-start.1
  80.6 0.0 copy-done
  80.6 1.9 %subtract_select_fusion = f32[12,64,128]{2,1,0:T(8,128)} fusion(f32[12,64,128]{2,1,0:T(8,128)S(1)} %copy-done, f32[12,64,128]{2,1,0:T(8,128)} %bitcast.13, pred[12]{0:T(512)(128)(4,1)S(1)} %iota_compare_fusion), kind=kLoop, calls=%fused_computation.1 | loop fusion | flops 196608 | bytes 1179660 | tf_op jit(solution)/shard_map/jit(_where)/select_n | solution.py:530
  82.5 0.0 copy-done.1
  82.5 1.1 %multiply_bitcast_fusion = f32[1,256,1024]{2,1,0:T(8,128)} fusion(f32[256,1024]{1,0:T(8,128)S(1)} %copy-done.1), kind=kLoop, calls=%fused_computation | loop fusion | flops 262144 | bytes 2097152 | tf_op jit(solution)/shard_map/mul | solution.py:531
  (1 shorter events, 0.0 us)
Async XLA Ops:
  1.3 79.3 %copy-start = (f32[12,64,128]{2,1,0:T(8,128)S(1)}, f32[12,64,128]{2,1,0:T(8,128)}, u32[]{:S(2)}) copy-start(f32[12,64,128]{2,1,0:T(8,128)} %param.8) | copy-start | bytes 1179652
  80.6 2.0 %copy-start.1 = (f32[256,1024]{1,0:T(8,128)S(1)}, f32[256,1024]{1,0:T(8,128)}, u32[]{:S(2)}) copy-start(f32[256,1024]{1,0:T(8,128)} %get-tuple-element.5) | copy-start | bytes 3145732

commit v7 on v6

--- a/solution.py
+++ b/solution.py
@@ -417,14 +417,10 @@
             )
             return carry
 
-        lax.fori_loop(0, nchunk, body, 0)
+        lax.fori_loop(0, nchunk, body, 0, unroll=2 if nchunk % 2 == 0 else 1)
 
     image(me)
-    for copy in z_copies:
-        copy.wait()
     o_copies = [pcopy(2, k, reso.at[f], reso.at[f]) for k in range(1, F)]
-    for copy in o_copies:
-        copy.start()
     for n in range(B - 1):
         if n == B - 2:
             for copy in o_copies:
@@ -441,6 +437,11 @@
         pl.when(me + 1 + n < B)(lambda n=n: left_(n).wait_recv())
         if n + 1 < B - 1:
             pl.when(sends_left(n + 1))(lambda n=n: left_(n + 1).start())
+        if n == 0:
+            for copy in z_copies:
+                copy.wait()
+            for copy in o_copies:
+                copy.start()
 
         def arrived(side, carry, n=n):
             src = jnp.where(side == 0, me - 1 - n, me + 1 + n)

time: 83.8 us -> 83.4 us (level)
  no operation moved by 1% of the time
where the time goes in v7:
time: 83.4 us; the launch traced here: 83.2 us
  Pallas kernels  78.8 us (94%)
  other arithmetic  3.07 us (4%)
  between operations  1.32 us (2%)
    pallas_call x1, Pallas kernels, per_device(): pl.pallas_call(functools.partial(kernel, dims), out_shape=(jax.ShapeDtype...  78.8 us
    select_n x1, other arithmetic, per_device(): residual = jnp.where(live, observed - predicted.reshape(TD, G, W), 0.0)  1.94 us

profile of v7, /device:TPU:0, one launch (start us, length us, event | category | flops | bytes accessed | tf_op | source)
XLA Modules:
  0.0 83.2 jit_solution(8589659504620944614)
XLA Ops:
  1.3 0.0 copy-start
  1.3 78.8 %shard_map.77 = (f32[256,1024]{1,0:T(8,128)}, f32[768,128]{1,0:T(8,128)}) custom-call(s32[2,12]{1,0:T(2,128)} %bitcast.14, s32[2,12]{1,0:T(2,128)} %bitcast.15, s32[1]{0:T(128)} %copy.8.counts_ref, bf16[256,1024]{1,0:T(8,128)(2,1)} %bitcast.12, bf16[64,64,128]{2,1,0:T(8,128)(2,1)} %bitcast.11, f32[768,128]{1,0:T(8,128)} %bitcast.10), custom_call_target="tpu_custom_call" | custom-call | tf_op jit(solution)/shard_map/pallas_call | solution.py:479
  80.1 0.0 copy-start.1
  80.1 0.0 copy-done
  80.1 1.9 %subtract_select_fusion = f32[12,64,128]{2,1,0:T(8,128)} fusion(f32[12,64,128]{2,1,0:T(8,128)S(1)} %copy-done, f32[12,64,128]{2,1,0:T(8,128)} %bitcast.13, pred[12]{0:T(512)(128)(4,1)S(1)} %iota_compare_fusion), kind=kLoop, calls=%fused_computation.1 | loop fusion | flops 196608 | bytes 1179660 | tf_op jit(solution)/shard_map/jit(_where)/select_n | solution.py:531
  82.1 0.0 copy-done.1
  82.1 1.1 %multiply_bitcast_fusion = f32[1,256,1024]{2,1,0:T(8,128)} fusion(f32[256,1024]{1,0:T(8,128)S(1)} %copy-done.1), kind=kLoop, calls=%fused_computation | loop fusion | flops 262144 | bytes 2097152 | tf_op jit(solution)/shard_map/mul | solution.py:532
  (1 shorter events, 0.0 us)
Async XLA Ops:
  1.3 78.8 %copy-start = (f32[12,64,128]{2,1,0:T(8,128)S(1)}, f32[12,64,128]{2,1,0:T(8,128)}, u32[]{:S(2)}) copy-start(f32[12,64,128]{2,1,0:T(8,128)} %param.8) | copy-start | bytes 1179652
  80.1 2.0 %copy-start.1 = (f32[256,1024]{1,0:T(8,128)S(1)}, f32[256,1024]{1,0:T(8,128)}, u32[]{:S(2)}) copy-start(f32[256,1024]{1,0:T(8,128)} %get-tuple-element.5) | copy-start | bytes 3145732
